TPU v7x, 32 devices: a whole 2x2x4 slice. The times are simulated.
32 devices in a mesh: lon: 4 (over x, core), lat: 4 (over z), tm: 2 (over y).
Axes of the slice: x: 2, y: 2, z: 4, core: 2. Of those that a mesh axis runs over, the one named last changes fastest.
Arguments:
- reanalysis: float32 [512, 128, 512], P('lon', 'lat', 'tm'), may hold values from 0.05 to 5
- lon_factor: float32 [64, 512], P(None, 'lon'), may hold values from 0.05 to 1
- lat_factor: float32 [64, 128], P(None, 'lat'), may hold values from 0.05 to 1
- time_factor: float32 [64, 512], P(None, 'tm'), may hold values from 0.05 to 1
Outputs:
- lon_updated: float32 [64, 512], P(None, 'lon')
- lat_updated: float32 [64, 128], P(None, 'lat')
- time_updated: float32 [64, 512], P(None, 'tm')
All inputs are finite; a program needn't handle non-finite values.
Results may differ from a plain program's by a relative error of at most 0.0003.
Values sent between devices are 32-bit elements; how exact they have to be, the bound alone decides.
A program may use at most 64 MiB of HBM per device.

v0:
```python
import jax
import jax.numpy as jnp
from jax import lax
from jax.sharding import PartitionSpec as P

EPSILON = 1e-06


def gram_of(factor):
    return jnp.dot(factor, factor.T, precision=lax.Precision.HIGHEST)


def hals(factor, terms, gram):
    rank = factor.shape[0]

    def update(index, current):
        grow = lax.dynamic_slice_in_dim(gram, index, 1, 0)
        pivot = lax.dynamic_slice_in_dim(grow, index, 1, 1)
        row = lax.dynamic_slice_in_dim(current, index, 1, 0)
        target = lax.dynamic_slice_in_dim(terms, index, 1, 0)
        change = (target - jnp.dot(grow, current, precision=lax.Precision.HIGHEST)) / pivot
        return lax.dynamic_update_slice_in_dim(
            current, jnp.maximum(row + change, EPSILON), index, 0
        )

    return lax.fori_loop(0, rank, update, factor)


def shards(reanalysis, lon_factor, lat_factor, time_factor):
    lon_rows, lat_rows, hr_rows = reanalysis.shape
    rank = lon_factor.shape[0]
    flat = reanalysis.reshape(lon_rows * lat_rows, hr_rows)
    inner = lax.dot_general(
        time_factor, flat, (((1,), (1,)), ((), ())), precision=lax.Precision.HIGHEST
    )
    inner = inner.reshape(rank, lon_rows, lat_rows)
    lon_part = jnp.sum(inner * lat_factor[:, None, :], axis=2)
    lat_gram = lax.psum(gram_of(lat_factor), "lat")
    time_gram = lax.psum(gram_of(time_factor), "tm")
    lon_terms = lax.psum(lon_part, ("lat", "tm"))
    lon_new = hals(lon_factor, lon_terms, lat_gram * time_gram)
    lon_gram = lax.psum(gram_of(lon_new), "lon")
    lat_part = jnp.sum(inner * lon_new[:, :, None], axis=1)
    lat_terms = lax.psum(lat_part, ("lon", "tm"))
    lat_new = hals(lat_factor, lat_terms, lon_gram * time_gram)
    lat_gram_new = lax.psum(gram_of(lat_new), "lat")
    pairs = (lon_new[:, :, None] * lat_new[:, None, :]).reshape(rank, lon_rows * lat_rows)
    time_part = jnp.dot(pairs, flat, precision=lax.Precision.HIGHEST)
    time_terms = lax.psum(time_part, ("lon", "lat"))
    time_new = hals(time_factor, time_terms, lon_gram * lat_gram_new)
    return (lon_new, lat_new, time_new)


def solution(mesh):
    in_specs = (P("lon", "lat", "tm"), P(None, "lon"), P(None, "lat"), P(None, "tm"))
    out_specs = (P(None, "lon"), P(None, "lat"), P(None, "tm"))
    return jax.shard_map(shards, mesh=mesh, in_specs=in_specs, out_specs=out_specs, check_vma=False)
```

profile of v0, /device:TPU:0, one launch (start us, length us, event | category | flops | bytes accessed | tf_op | source)
XLA Modules:
  0.0 532.7 jit_solution(4719006291266198136)
XLA Ops:
  10.1 8.5 %multiply_reduce_fusion.1 = (f32[64,128]{1,0:T(8,128)S(1)}, f32[64,128,32]{1,0,2:T(8,128)S(1)}) fusion(f32[64,32]{0,1:T(8,128)} %param.12, f32[128,32,256]{2,1,0:T(8,128)} %param.10, f32[64,256]{1,0:T(8,128)S(1)} %copy.51), kind=kOutput, calls=%fused_computation.29 | convolution fusion | flops 805822464 | bytes 5349376 | tf_op jit(solution)/shard_map/dot_general | solution.py:33
  18.6 38.9 %psum.49 = f32[64,128]{1,0:T(8,128)S(1)} all-reduce(f32[64,128]{1,0:T(8,128)S(1)} %get-tuple-element.416), channel_id=1, replica_groups=mesh['lon'=4,'lat'=4,'tm'=2] {'lat','tm'}, use_global_device_ids=true, to_apply=%region_3.0 | all-reduce | flops 8192 | bytes 65536 | tf_op jit(solution)/shard_map/psum | solution.py:40
  57.5 6.9 %psum.51 = f32[64,64]{1,0:T(8,128)S(1)} all-reduce(f32[64,64]{1,0:T(8,128)S(1)} %fusion.27), channel_id=1, replica_groups=mesh['lon'=4,'lat'=4,'tm'=2] {'tm'}, use_global_device_ids=true, to_apply=%region_1.0 | all-reduce | flops 4096 | bytes 32768 | tf_op jit(solution)/shard_map/psum | solution.py:39
  64.4 15.9 %psum.50 = f32[64,64]{1,0:T(8,128)S(1)} all-reduce(f32[64,64]{1,0:T(8,128)S(1)} %fusion.26), channel_id=1, replica_groups=mesh['lon'=4,'lat'=4,'tm'=2] {'lat'}, use_global_device_ids=true, to_apply=%region_0.0 | all-reduce | flops 4096 | bytes 32768 | tf_op jit(solution)/shard_map/psum | solution.py:38
  80.4 90.6 %while.48 = (s32[]{:T(128)}, f32[64,128]{1,0:T(8,128)S(1)}, f32[64,128]{1,0:T(8,128)S(1)}, f32[64,64]{1,0:T(8,128)S(1)}, s32[]{:T(128)}, /*index=5*/s32[]{:T(128)}, s32[]{:T(128)}) while((s32[]{:T(128)}, f32[64,128]{1,0:T(8,128)S(1)}, f32[64,128]{1,0:T(8,128)S(1)}, f32[64,64]{1,0:T(8,128)S(1)}, s32[]{:T(128)}, /*index=5*/s32[]{:T(128)}, ...), condition=%wide.region_5.0_spmd, body=%wide.region_4.0_spmd.sunk | while | flops 98819 | bytes 37485 | solution.py:26
  171.2 10.3 %psum.53 = f32[64,64]{1,0:T(8,128)S(1)} all-reduce(f32[64,64]{1,0:T(8,128)S(1)} %fusion.28), channel_id=1, replica_groups=mesh['lon'=4,'lat'=4,'tm'=2] {'lon'}, use_global_device_ids=true, to_apply=%region_6.0 | all-reduce | flops 4096 | bytes 32768 | tf_op jit(solution)/shard_map/psum | solution.py:42
  181.8 24.4 %psum.52 = f32[64,32]{0,1:T(8,128)S(1)} all-reduce(f32[64,32]{0,1:T(8,128)S(1)} %multiply_reduce_fusion), channel_id=1, replica_groups=mesh['lon'=4,'lat'=4,'tm'=2] {'lon','tm'}, use_global_device_ids=true, to_apply=%region_8.0 | all-reduce | flops 2048 | bytes 16384 | tf_op jit(solution)/shard_map/psum | solution.py:44
  206.3 90.6 %while.49 = (s32[]{:T(128)}, f32[64,32]{1,0:T(8,128)S(1)}, f32[64,32]{1,0:T(8,128)S(1)}, f32[64,64]{1,0:T(8,128)S(1)}, s32[]{:T(128)}, /*index=5*/s32[]{:T(128)}, s32[]{:T(128)}) while((s32[]{:T(128)}, f32[64,32]{1,0:T(8,128)S(1)}, f32[64,32]{1,0:T(8,128)S(1)}, f32[64,64]{1,0:T(8,128)S(1)}, s32[]{:T(128)}, /*index=5*/s32[]{:T(128)}, ...), condition=%wide.region_10.0_spmd, body=%wide.region_9.0_spmd.sunk | while | flops 24707 | bytes 36333 | solution.py:26
  297.0 7.4 %fusion.19 = f32[64,256]{1,0:T(8,128)} fusion(f32[128,32,256]{2,1,0:T(8,128)} %param.10, f32[64,32]{0,1:T(8,128)S(1)} %copy.17, f32[64,128]{1,0:T(8,128)S(1)} %get-tuple-element.389), kind=kOutput, calls=%fused_computation.26 | convolution fusion | flops 805568512 | bytes 4300800 | tf_op jit(solution)/shard_map/dot_general | solution.py:48
  304.7 17.6 %psum.55 = f32[64,64]{1,0:T(8,128)S(1)} all-reduce(f32[64,64]{1,0:T(8,128)S(1)} %fusion.29), channel_id=1, replica_groups=mesh['lon'=4,'lat'=4,'tm'=2] {'lat'}, use_global_device_ids=true, to_apply=%region_11.0 | all-reduce | flops 4096 | bytes 32768 | tf_op jit(solution)/shard_map/psum | solution.py:46
  322.3 65.2 %all-reduce.2.cloned.1.call-done = f32[64,256]{1,0:T(8,128)} async-done(((f32[64,256]{1,0:T(8,128)}), f32[64,256]{1,0:T(8,128)}) %all-reduce.2.cloned.1.call-update) | async-done | bytes 65552 | tf_op jit(solution)/shard_map/psum | solution.py:49
  387.5 137.7 %while.50 = (s32[]{:T(128)}, f32[64,256]{1,0:T(8,128)S(1)}, f32[64,256]{1,0:T(8,128)}, f32[64,64]{1,0:T(8,128)S(1)}, s32[]{:T(128)}, /*index=5*/s32[]{:T(128)}, s32[]{:T(128)}) while((s32[]{:T(128)}, f32[64,256]{1,0:T(8,128)S(1)}, f32[64,256]{1,0:T(8,128)}, f32[64,64]{1,0:T(8,128)S(1)}, s32[]{:T(128)}, /*index=5*/s32[]{:T(128)}, ...), condition=%wide.region_14.0_spmd, body=%wide.region_13.0_spmd.sunk | while | flops 197635 | bytes 72813 | solution.py:26
  388.1 1.5 fusion.58
  390.2 1.5 fusion.58
  392.4 1.5 fusion.58
  394.5 1.5 fusion.58
  396.7 1.5 fusion.58
  398.8 1.5 fusion.58
  401.0 1.5 fusion.58
  403.1 1.5 fusion.58
  405.3 1.5 fusion.58
  407.4 1.5 fusion.58
  409.6 1.5 fusion.58
  411.7 1.5 fusion.58
  413.9 1.5 fusion.58
  416.0 1.5 fusion.58
  422.5 1.5 fusion.58
  424.7 1.5 fusion.58
  426.8 1.5 fusion.58
  429.0 1.5 fusion.58
  431.1 1.5 fusion.58
  433.3 1.5 fusion.58
  435.4 1.5 fusion.58
  437.6 1.5 fusion.58
  441.9 1.5 fusion.58
  444.0 1.5 fusion.58
  446.2 1.5 fusion.58
  450.5 1.5 fusion.58
  452.6 1.5 fusion.58
  459.1 1.5 fusion.58
  461.2 1.5 fusion.58
  465.6 1.5 fusion.58
  467.7 1.5 fusion.58
  469.9 1.5 fusion.58
  474.2 1.5 fusion.58
  476.3 1.5 fusion.58
  478.5 1.5 fusion.58
  482.8 1.5 fusion.58
  484.9 1.5 fusion.58
  487.1 1.5 fusion.58
  491.4 1.5 fusion.58
  493.5 1.5 fusion.58
  495.7 1.5 fusion.58
  497.8 1.5 fusion.58
  500.0 1.5 fusion.58
  502.1 1.5 fusion.58
  504.3 1.5 fusion.58
  506.4 1.5 fusion.58
  510.8 1.5 fusion.58
  512.9 1.5 fusion.58
  515.1 1.5 fusion.58
  519.4 1.5 fusion.58
  521.5 1.5 fusion.58
  523.7 1.5 fusion.58
  (546 shorter events, 241.6 us)
Async XLA Ops:
  7.2 73.2 %copy-start.2 = (f32[64,128]{1,0:T(8,128)S(1)}, f32[64,128]{1,0:T(8,128)}, u32[]{:S(2)}) copy-start(f32[64,128]{1,0:T(8,128)} %param.11) | copy-start | bytes 98308
  7.2 380.3 %all-reduce.2.cloned.1.call-start = ((), (), s32[]{:S(2)}) async-start(), calls=%async_computation | async-start | bytes 131072 | tf_op jit(solution)/shard_map/psum | solution.py:49
  171.0 354.2 %copy-start.1 = (f32[64,128]{1,0:T(8,128)}, f32[64,128]{1,0:T(8,128)S(1)}, u32[]{:S(2)}) copy-start(f32[64,128]{1,0:T(8,128)S(1)} %get-tuple-element.389) | copy-start | bytes 98308
  297.0 228.2 %copy-start.3 = (f32[64,32]{0,1:T(8,128)}, f32[64,32]{0,1:T(8,128)S(1)}, u32[]{:S(2)}) copy-start(f32[64,32]{0,1:T(8,128)S(1)} %copy.17) | copy-start | bytes 24580
  525.2 0.6 copy-start
Sparse Core Ops, SparseCore 0:
  304.6 82.8 all-reduce.1
where the time goes:
time: 539 us; the launch traced here: 533 us
  matrix products  213 us (40%)
  local copies, waits for them, and re-layouts  121 us (22%)
  blocking collectives  114 us (21%)
  waiting for transfers between devices  65.2 us (12%)
  between operations  14.2 us (3%)
    dot_general x192, matrix products, update(): jnp.dot(grow, current, precision=lax.Precision.HIGHEST)  196 us
    dynamic_slice x192, local copies, waits for them, and re-layouts, update(): pivot = lax.dynamic_slice_in_dim(grow, index, 1, 1)  113 us
    psum x1, waiting for transfers between devices, shards(): time_terms = lax.psum(time_part, ('lon', 'lat'))  65.2 us
    psum x1, blocking collectives, shards(): lon_terms = lax.psum(lon_part, ('lat', 'tm'))  38.9 us
    psum x1, blocking collectives, shards(): lat_terms = lax.psum(lat_part, ('lon', 'tm'))  24.4 us
    psum x1, blocking collectives, shards(): lat_gram_new = lax.psum(gram_of(lat_new), 'lat')  17.6 us
    psum x1, blocking collectives, shards(): lat_gram = lax.psum(gram_of(lat_factor), 'lat')  15.9 us
  transfers between devices with their start and end apart: 1, of which 1 were waited for; matrix products, arithmetic and copies ran while one was open for 0% of the time, Pallas kernels for 0%

commit v1 on v0

v1 whole, which is shorter than its diff:
```python
import functools

import jax
import jax.numpy as jnp
from jax import lax
from jax.experimental import pallas as pl
from jax.experimental.pallas import tpu as pltpu
from jax.sharding import PartitionSpec as P

EPSILON = 1e-06
MESH = pl.DeviceIdType.MESH
SUB = 8
LANE = 128


def gram_of(factor):
    return lax.dot_general(
        factor, factor, (((1,), (1,)), ((), ())),
        precision=lax.Precision.HIGHEST, preferred_element_type=jnp.float32,
    )


def halves(value):
    high = value.astype(jnp.bfloat16)
    return high, (value - high.astype(jnp.float32)).astype(jnp.bfloat16)


def widen(value, rows, cols):
    r, c = value.shape
    if c < cols:
        value = jnp.concatenate([value, jnp.zeros((r, cols - c), value.dtype)], axis=1)
    if r < rows:
        value = jnp.concatenate([value, jnp.zeros((rows - r, cols), value.dtype)], axis=0)
    return value


def turn(value):
    r, c = value.shape
    full = widen(value, -(-r // LANE) * LANE, -(-c // LANE) * LANE)
    return full.T[:c, :r]


def hals(out_ref, factor, terms, gram):
    rank = factor.shape[0]
    row = lax.broadcasted_iota(jnp.int32, (rank, rank), 0)
    col = lax.broadcasted_iota(jnp.int32, (rank, rank), 1)
    inverse = 1.0 / jnp.sum(jnp.where(row == col, gram, 0.0), axis=1, keepdims=True)
    scaled = gram * inverse
    rest = (terms - jnp.dot(gram, factor, precision=lax.Precision.HIGHEST,
                            preferred_element_type=jnp.float32)) * inverse
    for r in range(rank):
        old = factor[r:r + 1]
        new = jnp.maximum(old + rest[r:r + 1], EPSILON)
        out_ref[r:r + 1, :] = new
        if r < rank - 1:
            rest = rest - scaled[:, r:r + 1] * (new - old)


class Group:
    def __init__(self, sizes, axes):
        self.axes = axes
        self.sizes = [sizes[a] for a in axes]
        self.count = 1
        for s in self.sizes:
            self.count *= s

    def me(self):
        index = 0
        for a, s in zip(self.axes, self.sizes):
            index = index * s + lax.axis_index(a)
        return index

    def device(self, index):
        place = {}
        for a, s in reversed(list(zip(self.axes, self.sizes))):
            place[a] = lax.rem(index, s)
            index = lax.div(index, s)
        return place

    def peer(self, offset):
        return lax.rem(self.me() + offset, self.count)

    def source(self, offset):
        return lax.rem(self.me() + (self.count - offset), self.count)


def when(condition, action):
    if condition is True:
        action()
    else:
        pl.when(condition)(action)


class Share:
    def __init__(self, group, slots, send, recv):
        self.group, self.slots = group, slots
        self.copies = []
        me = group.me()
        for o in range(1, group.count):
            self.copies.append(pltpu.make_async_remote_copy(
                src_ref=slots.at[me], dst_ref=slots.at[me],
                send_sem=send.at[o - 1], recv_sem=recv.at[o - 1],
                device_id=group.device(group.peer(o)), device_id_type=MESH))

    def start(self, value):
        self.slots[self.group.me()] = value
        for copy in self.copies:
            copy.start()

    def finish(self):
        for copy in self.copies:
            copy.wait()
        total = self.slots[0]
        for i in range(1, self.group.count):
            total = total + self.slots[i]
        return total


class Reduce:
    def __init__(self, group, part, slots, final, send1, recv1, send2, recv2):
        self.group, self.part, self.slots, self.final = group, part, slots, final
        pieces = part.shape[0]
        self.owners = min(group.count, pieces)
        self.per = pieces // self.owners
        self.all_own = self.owners == group.count
        me = group.me()
        self.scatter, self.gather = [], []
        for o in range(1, group.count):
            to = group.peer(o)
            device = group.device(to)
            self.scatter.append(pltpu.make_async_remote_copy(
                src_ref=part.at[self.tiles(to)], dst_ref=slots.at[o - 1],
                send_sem=send1.at[o - 1], recv_sem=recv1.at[o - 1],
                device_id=device, device_id_type=MESH))
            self.gather.append(pltpu.make_async_remote_copy(
                src_ref=final.at[self.tiles(me)], dst_ref=final.at[self.tiles(me)],
                send_sem=send2.at[o - 1], recv_sem=recv2.at[o - 1],
                device_id=device, device_id_type=MESH))

    def owns(self, index):
        return True if self.all_own else index < self.owners

    def tiles(self, index):
        if not self.all_own:
            index = jnp.minimum(index, self.owners - 1)
        return pl.ds(index * self.per, self.per)

    def start(self, value):
        for i in range(value.shape[1] // LANE):
            rows = value.shape[0] // SUB
            self.part[i * rows:(i + 1) * rows] = value[:, i * LANE:(i + 1) * LANE].reshape(rows, SUB, LANE)
        for o, copy in enumerate(self.scatter, 1):
            when(self.owns(self.group.peer(o)), copy.start)

    def middle(self):
        me = self.group.me()

        def add():
            for copy in self.scatter:
                copy.wait_recv()
            total = self.part[self.tiles(me)]
            for o in range(1, self.group.count):
                total = total + self.slots[o - 1]
            self.final[self.tiles(me)] = total
            for copy in self.gather:
                copy.start()

        when(self.owns(me), add)

    def finish(self, rank):
        me = self.group.me()
        for o, copy in enumerate(self.gather, 1):
            when(self.owns(self.group.source(o)), copy.wait_recv)
        rows = rank // SUB
        pieces = self.part.shape[0]
        tiles = [self.final[i:i + rows].reshape(rank, LANE) for i in range(0, pieces, rows)]
        return tiles[0] if len(tiles) == 1 else jnp.concatenate(tiles, axis=1)

    def drain(self):
        for o, copy in enumerate(self.scatter, 1):
            when(self.owns(self.group.peer(o)), copy.wait_send)

        def sent():
            for copy in self.gather:
                copy.wait_send()

        when(self.owns(self.group.me()), sent)


def kernel(sizes, shape, x_ref, lon_ref, lat_ref, time_ref, lon_out, lat_out, time_out,
           xh, xl, inner, lon_t, *comm):
    n_lon, n_lat, n_hr = shape
    rank = lon_ref.shape[0]
    lon_axis, lat_axis, tm_axis = (Group(sizes, (a,)) for a in ("lon", "lat", "tm"))
    lat_tm, lon_tm, lon_lat = Group(sizes, ("lat", "tm")), Group(sizes, ("lon", "tm")), Group(sizes, ("lon", "lat"))

    barrier = pltpu.get_barrier_semaphore()
    signals = 0
    for group in (lat_tm, lon_tm, lon_lat):
        for o in range(1, group.count):
            pl.semaphore_signal(barrier, inc=1, device_id=group.device(group.peer(o)), device_id_type=MESH)
            signals += 1
    pl.semaphore_wait(barrier, signals)

    lat_gram = Share(lat_axis, *comm[0:3])
    time_gram = Share(tm_axis, *comm[3:6])
    lon_gram = Share(lon_axis, *comm[6:9])
    lat_gram_new = Share(lat_axis, *comm[9:12])
    lon_sum = Reduce(lat_tm, *comm[12:19])
    lat_sum = Reduce(lon_tm, *comm[19:26])
    time_sum = Reduce(lon_lat, *comm[26:33])

    lat_gram.start(gram_of(lat_ref[...]))
    time_gram.start(gram_of(time_ref[...]))

    step = 16
    chunk = step * n_lat
    weights = jnp.concatenate(halves(time_ref[...]), axis=0)
    lat_t = turn(lat_ref[...])

    def first(c, _):
        rows = pl.ds(pl.multiple_of(c * chunk, chunk), chunk)
        high, low = halves(x_ref[rows, :])
        xh[rows, :] = high
        xl[rows, :] = low
        nt = (((1,), (1,)), ((), ()))
        both = lax.dot_general(high, weights, nt, preferred_element_type=jnp.float32)
        both = both + lax.dot_general(low, weights, nt, preferred_element_type=jnp.float32)
        value = both[:, :rank] + both[:, rank:]
        inner[rows, :] = value
        lon_t[pl.ds(pl.multiple_of(c * step, step), step), :] = jnp.sum(
            value.reshape(step, n_lat, rank) * lat_t[None], axis=1)
        return 0

    lax.fori_loop(0, n_lon // step, first, 0)
    lon_sum.start(turn(lon_t[...]))
    lon_sum.middle()
    time_g = time_gram.finish()
    gram = lat_gram.finish() * time_g
    hals(lon_out, lon_ref[...], lon_sum.finish(rank), gram)

    lon_new = lon_out[...]
    lon_gram.start(gram_of(lon_new))
    lon_t[...] = turn(lon_new)

    def second(c, total):
        rows = pl.ds(pl.multiple_of(c * chunk, chunk), chunk)
        scale = lon_t[pl.ds(pl.multiple_of(c * step, step), step), :]
        return total + jnp.sum(inner[rows, :].reshape(step, n_lat, rank) * scale[:, None, :], axis=0)

    lat_part = lax.fori_loop(0, n_lon // step, second, jnp.zeros((n_lat, rank), jnp.float32))
    lat_sum.start(widen(turn(lat_part), rank, -(-n_lat // LANE) * LANE))
    lat_sum.middle()
    lon_g = lon_gram.finish()
    gram = lon_g * time_g
    hals(lat_out, lat_ref[...], lat_sum.finish(rank)[:, :n_lat], gram)

    lat_new = lat_out[...]
    lat_gram_new.start(gram_of(lat_new))
    lat_t = turn(lat_new)

    def third(c, total):
        rows = pl.ds(pl.multiple_of(c * chunk, chunk), chunk)
        scale = lon_t[pl.ds(pl.multiple_of(c * step, step), step), :]
        pairs = (scale[:, None, :] * lat_t[None]).reshape(chunk, rank)
        high = pairs.astype(jnp.bfloat16).astype(jnp.float32)
        both = jnp.concatenate([high, pairs - high], axis=1).T.astype(jnp.bfloat16)
        total = total + jnp.dot(both, xh[rows, :], preferred_element_type=jnp.float32)
        return total + jnp.dot(both, xl[rows, :], preferred_element_type=jnp.float32)

    both = lax.fori_loop(0, n_lon // step, third, jnp.zeros((2 * rank, n_hr), jnp.float32))
    time_sum.start(both[:rank] + both[rank:])
    time_sum.middle()
    gram = lon_g * lat_gram_new.finish()
    hals(time_out, time_ref[...], time_sum.finish(rank), gram)
    for part in (lon_sum, lat_sum, time_sum):
        part.drain()


def shards(sizes, reanalysis, lon_factor, lat_factor, time_factor):
    n_lon, n_lat, n_hr = reanalysis.shape
    rank = lon_factor.shape[0]
    cells = n_lon * n_lat
    flat = reanalysis.reshape(cells, n_hr)

    def sems(count):
        return [pltpu.SemaphoreType.DMA((max(count - 1, 1),))] * 2

    def share(count):
        return [pltpu.VMEM((count, rank, rank), jnp.float32)] + sems(count)

    def reduce(count, columns):
        pieces = rank // SUB * -(-columns // LANE)
        per = pieces // min(count, pieces)
        return [
            pltpu.VMEM((pieces, SUB, LANE), jnp.float32),
            pltpu.VMEM((max(count - 1, 1), per, SUB, LANE), jnp.float32),
            pltpu.VMEM((pieces, SUB, LANE), jnp.float32),
        ] + sems(count) + sems(count)

    lon, lat, tm = sizes["lon"], sizes["lat"], sizes["tm"]
    comm = share(lat) + share(tm) + share(lon) + share(lat)
    comm += reduce(lat * tm, n_lon) + reduce(lon * tm, n_lat) + reduce(lon * lat, n_hr)
    return pl.pallas_call(
        functools.partial(kernel, sizes, (n_lon, n_lat, n_hr)),
        out_shape=[jax.ShapeDtypeStruct(f.shape, jnp.float32) for f in (lon_factor, lat_factor, time_factor)],
        in_specs=[pl.BlockSpec(memory_space=pltpu.VMEM)] * 4,
        out_specs=[pl.BlockSpec(memory_space=pltpu.VMEM)] * 3,
        scratch_shapes=[
            pltpu.VMEM((cells, n_hr), jnp.bfloat16),
            pltpu.VMEM((cells, n_hr), jnp.bfloat16),
            pltpu.VMEM((cells, rank), jnp.float32),
            pltpu.VMEM((n_lon, rank), jnp.float32),
        ] + comm,
        compiler_params=pltpu.CompilerParams(
            collective_id=0, has_side_effects=True, vmem_limit_bytes=40 * 1024 * 1024),
    )(flat, lon_factor, lat_factor, time_factor)


def solution(mesh):
    sizes = dict(mesh.shape)
    in_specs = (P("lon", "lat", "tm"), P(None, "lon"), P(None, "lat"), P(None, "tm"))
    out_specs = (P(None, "lon"), P(None, "lat"), P(None, "tm"))

    def run(*args):
        return tuple(shards(sizes, *args))

    return jax.shard_map(run, mesh=mesh, in_specs=in_specs, out_specs=out_specs, check_vma=False)
```

time: 539 us -> 47.6 us (0.09); the launches traced: 533 us -> 47.3 us
  matrix products: 213 us -> 0 us
  local copies, waits for them, and re-layouts: 121 us -> 6.51 us
  blocking collectives: 114 us -> 0 us
  waiting for transfers between devices: 65.2 us -> 0 us
  Pallas kernels: 0 us -> 40.1 us
  between operations: 14.2 us -> 0.65 us
    dot_general x198 -> x0, matrix products: 213 us -> none  [the longest x192 196 us: update(): jnp.dot(grow, current, precision=lax.Precision.HIGHEST)]
    psum x6 -> x0, blocking collectives: 114 us -> none  [the longest x1 38.9 us: shards(): lon_terms = lax.psum(lon_part, ('lat', 'tm'))]
    dynamic_slice x192 -> x0, local copies, waits for them, and re-layouts: 113 us -> none  [update(): pivot = lax.dynamic_slice_in_dim(grow, index, 1, 1)]
    psum x1 -> x0, waiting for transfers between devices: 65.2 us -> none  [shards(): time_terms = lax.psum(time_part, ('lon', 'lat'))]
    pallas_call x0 -> x1, Pallas kernels: none -> 40.1 us  [shards(): pl.pallas_call(functools.partial(kernel, sizes, (n_lon, n_lat, n_hr)), ou...]
    dynamic_update_slice x192 -> x0, local copies, waits for them, and re-layouts: 6 us -> none  [update(): lax.dynamic_update_slice_in_dim(current, jnp.maximum(row + change, EPSILO...]
  transfers between devices with their start and end apart: 1 -> 0, of which waited for: 1 -> 0; matrix products, arithmetic and copies ran while one was open for 0% -> 0% of each run, Pallas kernels for 0% -> 0%
where the time goes in v1:
time: 47.6 us; the launch traced here: 47.3 us
  Pallas kernels  40.1 us (84%)
  local copies, waits for them, and re-layouts  6.51 us (14%)
  between operations  0.65 us (1%)
    pallas_call x1, Pallas kernels, shards(): pl.pallas_call(functools.partial(kernel, sizes, (n_lon, n_lat, n_hr)), ou...  40.1 us
    unnamed x9, local copies, waits for them, and re-layouts  5.83 us

profile of v1, /device:TPU:0, one launch (start us, length us, event | category | flops | bytes accessed | tf_op | source)
XLA Modules:
  0.0 47.3 jit_solution(8707876679349518645)
XLA Ops:
  0.6 0.8 %copy.7.lat_ref = f32[64,32]{1,0:T(8,128)S(1)} copy(f32[64,32]{0,1:T(8,128)} %param.6) | data formatting | bytes 16384 | tf_op args[2]
  1.4 0.0 copy-start
  1.4 2.2 %copy-done = f32[128,32,256]{2,1,0:T(8,128)S(1)} copy-done((f32[128,32,256]{2,1,0:T(8,128)S(1)}, f32[128,32,256]{2,1,0:T(8,128)}, u32[]{:S(2)}) %copy-start) | copy-done | bytes 4194328
  3.6 0.0 copy-start.1
  3.6 0.8 %copy-done.1 = f32[64,256]{1,0:T(8,128)S(1)} copy-done((f32[64,256]{1,0:T(8,128)S(1)}, f32[64,256]{1,0:T(8,128)}, u32[]{:S(2)}) %copy-start.1) | copy-done | bytes 65560
  4.5 0.0 copy-start.2
  4.5 0.8 %copy-done.2 = f32[64,128]{1,0:T(8,128)S(1)} copy-done((f32[64,128]{1,0:T(8,128)S(1)}, f32[64,128]{1,0:T(8,128)}, u32[]{:S(2)}) %copy-start.2) | copy-done | bytes 32792
  5.2 40.1 %shard_map.67 = (f32[64,128]{1,0:T(8,128)S(1)}, f32[64,32]{1,0:T(8,128)S(1)}, f32[64,256]{1,0:T(8,128)S(1)}) custom-call(f32[4096,256]{1,0:T(8,128)S(1)} %bitcast.1, f32[64,128]{1,0:T(8,128)S(1)} %copy-done.2, f32[64,32]{1,0:T(8,128)S(1)} %copy.7.lat_ref, f32[64,256]{1,0:T(8,128)S(1)} %copy-done.1), custom_call_target="tpu_custom_call" | custom-call | tf_op jit(solution)/shard_map/pallas_call | solution.py:304
  45.4 0.7 %copy.8 = f32[64,32]{0,1:T(8,128)} copy(f32[64,32]{1,0:T(8,128)S(1)} %get-tuple-element.4) | data formatting | bytes 16384 | tf_op jit(solution)/shard_map/pallas_call | solution.py:304
  46.0 0.6 %copy.11 = f32[64,128]{1,0:T(8,128)} copy(f32[64,128]{1,0:T(8,128)S(1)} %get-tuple-element.9) | data formatting | bytes 65536
  46.6 0.6 %copy.12 = f32[64,256]{1,0:T(8,128)} copy(f32[64,256]{1,0:T(8,128)S(1)} %get-tuple-element.11) | data formatting | bytes 131072
Async XLA Ops:
  1.4 2.2 %copy-start = (f32[128,32,256]{2,1,0:T(8,128)S(1)}, f32[128,32,256]{2,1,0:T(8,128)}, u32[]{:S(2)}) copy-start(f32[128,32,256]{2,1,0:T(8,128)} %param.4) | copy-start | bytes 12582916
  3.6 0.8 %copy-start.1 = (f32[64,256]{1,0:T(8,128)S(1)}, f32[64,256]{1,0:T(8,128)}, u32[]{:S(2)}) copy-start(f32[64,256]{1,0:T(8,128)} %time_ref.1) | copy-start | bytes 196612
  4.5 0.8 %copy-start.2 = (f32[64,128]{1,0:T(8,128)S(1)}, f32[64,128]{1,0:T(8,128)}, u32[]{:S(2)}) copy-start(f32[64,128]{1,0:T(8,128)} %lon_ref.1) | copy-start | bytes 98308

commit v2 on v1

--- a/solution.py
+++ b/solution.py
@@ -56,6 +56,17 @@
             rest = rest - scaled[:, r:r + 1] * (new - old)
 
 
+def pack(value, lanes=LANE):
+    rows, cols = value.shape
+    blocks = max(lanes // cols, 1)
+    step = rows // blocks
+    return jnp.concatenate([value[i * step:(i + 1) * step] for i in range(blocks)], axis=1)
+
+
+def unpack(value, cols):
+    return jnp.concatenate([value[:, i:i + cols] for i in range(0, value.shape[1], cols)], axis=0)
+
+
 class Group:
     def __init__(self, sizes, axes):
         self.axes = axes
@@ -103,17 +114,17 @@
                 device_id=group.device(group.peer(o)), device_id_type=MESH))
 
     def start(self, value):
-        self.slots[self.group.me()] = value
+        self.slots[self.group.me()] = pack(value)
         for copy in self.copies:
             copy.start()
 
-    def finish(self):
+    def finish(self, cols):
         for copy in self.copies:
             copy.wait()
         total = self.slots[0]
         for i in range(1, self.group.count):
             total = total + self.slots[i]
-        return total
+        return unpack(total, cols)
 
 
 class Reduce:
@@ -187,10 +198,23 @@
         when(self.owns(self.group.me()), sent)
 
 
-def kernel(sizes, shape, x_ref, lon_ref, lat_ref, time_ref, lon_out, lat_out, time_out,
-           xh, xl, inner, lon_t, *comm):
+def kernel(sizes, shape, x_hbm, lon_hbm, lat_hbm, time_hbm, lon_out, lat_out, time_out,
+           x_ref, lon_ref, lat_ref, time_ref, load, x_load, xh, xl, inner, lon_t, lat_new_ref, *comm):
     n_lon, n_lat, n_hr = shape
     rank = lon_ref.shape[0]
+    step = 16
+    chunk = step * n_lat
+    small = [pltpu.make_async_copy(src, dst, load.at[i]) for i, (src, dst) in enumerate(
+        ((time_hbm, time_ref), (lat_hbm, lat_ref), (lon_hbm, lon_ref)))]
+
+    def piece(c):
+        rows = pl.ds(pl.multiple_of(c * chunk, chunk), chunk)
+        return pltpu.make_async_copy(x_hbm.at[rows], x_ref.at[rows], x_load.at[c])
+
+    for copy in small:
+        copy.start()
+    for c in range(n_lon // step):
+        piece(c).start()
     lon_axis, lat_axis, tm_axis = (Group(sizes, (a,)) for a in ("lon", "lat", "tm"))
     lat_tm, lon_tm, lon_lat = Group(sizes, ("lat", "tm")), Group(sizes, ("lon", "tm")), Group(sizes, ("lon", "lat"))
 
@@ -200,26 +224,27 @@
         for o in range(1, group.count):
             pl.semaphore_signal(barrier, inc=1, device_id=group.device(group.peer(o)), device_id_type=MESH)
             signals += 1
-    pl.semaphore_wait(barrier, signals)
+
+    for copy in small:
+        copy.wait()
 
     lat_gram = Share(lat_axis, *comm[0:3])
     time_gram = Share(tm_axis, *comm[3:6])
     lon_gram = Share(lon_axis, *comm[6:9])
     lat_gram_new = Share(lat_axis, *comm[9:12])
     lon_sum = Reduce(lat_tm, *comm[12:19])
-    lat_sum = Reduce(lon_tm, *comm[19:26])
-    time_sum = Reduce(lon_lat, *comm[26:33])
-
-    lat_gram.start(gram_of(lat_ref[...]))
-    time_gram.start(gram_of(time_ref[...]))
-
-    step = 16
-    chunk = step * n_lat
+    lat_sum = Share(lon_tm, *comm[19:22])
+    time_sum = Reduce(lon_lat, *comm[22:29])
+
     weights = jnp.concatenate(halves(time_ref[...]), axis=0)
-    lat_t = turn(lat_ref[...])
+    lat_t = lat_ref[...]
+    lat_old = turn(lat_t)
+    lat_start = gram_of(lat_old)
+    time_start = gram_of(time_ref[...])
 
     def first(c, _):
         rows = pl.ds(pl.multiple_of(c * chunk, chunk), chunk)
+        piece(c).wait()
         high, low = halves(x_ref[rows, :])
         xh[rows, :] = high
         xl[rows, :] = low
@@ -233,10 +258,15 @@
         return 0
 
     lax.fori_loop(0, n_lon // step, first, 0)
-    lon_sum.start(turn(lon_t[...]))
+    lon_part = turn(lon_t[...])
+    if signals:
+        pl.semaphore_wait(barrier, signals)
+    lon_sum.start(lon_part)
+    lat_gram.start(lat_start)
+    time_gram.start(time_start)
     lon_sum.middle()
-    time_g = time_gram.finish()
-    gram = lat_gram.finish() * time_g
+    time_g = time_gram.finish(rank)
+    gram = lat_gram.finish(rank) * time_g
     hals(lon_out, lon_ref[...], lon_sum.finish(rank), gram)
 
     lon_new = lon_out[...]
@@ -249,15 +279,15 @@
         return total + jnp.sum(inner[rows, :].reshape(step, n_lat, rank) * scale[:, None, :], axis=0)
 
     lat_part = lax.fori_loop(0, n_lon // step, second, jnp.zeros((n_lat, rank), jnp.float32))
-    lat_sum.start(widen(turn(lat_part), rank, -(-n_lat // LANE) * LANE))
-    lat_sum.middle()
-    lon_g = lon_gram.finish()
+    lat_sum.start(turn(lat_part))
+    lon_g = lon_gram.finish(rank)
     gram = lon_g * time_g
-    hals(lat_out, lat_ref[...], lat_sum.finish(rank)[:, :n_lat], gram)
-
-    lat_new = lat_out[...]
+    hals(lat_new_ref, lat_old, lat_sum.finish(n_lat), gram)
+
+    lat_new = lat_new_ref[...]
     lat_gram_new.start(gram_of(lat_new))
     lat_t = turn(lat_new)
+    lat_out[...] = lat_t
 
     def third(c, total):
         rows = pl.ds(pl.multiple_of(c * chunk, chunk), chunk)
@@ -271,9 +301,9 @@
     both = lax.fori_loop(0, n_lon // step, third, jnp.zeros((2 * rank, n_hr), jnp.float32))
     time_sum.start(both[:rank] + both[rank:])
     time_sum.middle()
-    gram = lon_g * lat_gram_new.finish()
+    gram = lon_g * lat_gram_new.finish(rank)
     hals(time_out, time_ref[...], time_sum.finish(rank), gram)
-    for part in (lon_sum, lat_sum, time_sum):
+    for part in (lon_sum, time_sum):
         part.drain()
 
 
@@ -286,8 +316,9 @@
     def sems(count):
         return [pltpu.SemaphoreType.DMA((max(count - 1, 1),))] * 2
 
-    def share(count):
-        return [pltpu.VMEM((count, rank, rank), jnp.float32)] + sems(count)
+    def share(count, columns=rank):
+        blocks = max(LANE // columns, 1)
+        return [pltpu.VMEM((count, rank // blocks, blocks * columns), jnp.float32)] + sems(count)
 
     def reduce(count, columns):
         pieces = rank // SUB * -(-columns // LANE)
@@ -300,21 +331,30 @@
 
     lon, lat, tm = sizes["lon"], sizes["lat"], sizes["tm"]
     comm = share(lat) + share(tm) + share(lon) + share(lat)
-    comm += reduce(lat * tm, n_lon) + reduce(lon * tm, n_lat) + reduce(lon * lat, n_hr)
-    return pl.pallas_call(
+    comm += reduce(lat * tm, n_lon) + share(lon * tm, n_lat) + reduce(lon * lat, n_hr)
+    lat_turned = lat_factor.T
+    lon_new, lat_new, time_new = pl.pallas_call(
         functools.partial(kernel, sizes, (n_lon, n_lat, n_hr)),
-        out_shape=[jax.ShapeDtypeStruct(f.shape, jnp.float32) for f in (lon_factor, lat_factor, time_factor)],
-        in_specs=[pl.BlockSpec(memory_space=pltpu.VMEM)] * 4,
+        out_shape=[jax.ShapeDtypeStruct(f.shape, jnp.float32) for f in (lon_factor, lat_turned, time_factor)],
+        in_specs=[pl.BlockSpec(memory_space=pltpu.HBM)] * 4,
         out_specs=[pl.BlockSpec(memory_space=pltpu.VMEM)] * 3,
         scratch_shapes=[
+            pltpu.VMEM(flat.shape, jnp.float32),
+            pltpu.VMEM(lon_factor.shape, jnp.float32),
+            pltpu.VMEM(lat_turned.shape, jnp.float32),
+            pltpu.VMEM(time_factor.shape, jnp.float32),
+            pltpu.SemaphoreType.DMA((3,)),
+            pltpu.SemaphoreType.DMA((n_lon // 16,)),
             pltpu.VMEM((cells, n_hr), jnp.bfloat16),
             pltpu.VMEM((cells, n_hr), jnp.bfloat16),
             pltpu.VMEM((cells, rank), jnp.float32),
             pltpu.VMEM((n_lon, rank), jnp.float32),
+            pltpu.VMEM(lat_factor.shape, jnp.float32),
         ] + comm,
         compiler_params=pltpu.CompilerParams(
             collective_id=0, has_side_effects=True, vmem_limit_bytes=40 * 1024 * 1024),
-    )(flat, lon_factor, lat_factor, time_factor)
+    )(flat, lon_factor, lat_turned, time_factor)
+    return lon_new, lat_new.T, time_new
 
 
 def solution(mesh):

time: 47.6 us -> 42 us (0.88)
  Pallas kernels: 40.1 us -> 34.7 us
    pallas_call x1, Pallas kernels: 40.1 us -> 34.7 us  [shards(): pl.pallas_call(functools.partial(kernel, sizes, (n_lon, n_lat, n_hr)), ou...]
    pallas_call x1 -> x0, local copies, waits for them, and re-layouts: 0.68 us -> none  [shards(): pl.pallas_call(functools.partial(kernel, sizes, (n_lon, n_lat, n_hr)), ou...]
    unnamed x9 -> x11, local copies, waits for them, and re-layouts: 5.83 us -> 6.35 us
where the time goes in v2:
time: 42 us; the launch traced here: 41.7 us
  Pallas kernels  34.7 us (83%)
  local copies, waits for them, and re-layouts  6.35 us (15%)
  between operations  0.65 us (2%)
    pallas_call x1, Pallas kernels, shards(): pl.pallas_call(functools.partial(kernel, sizes, (n_lon, n_lat, n_hr)), ou...  34.7 us
    unnamed x11, local copies, waits for them, and re-layouts  6.35 us

profile of v2, /device:TPU:0, one launch (start us, length us, event | category | flops | bytes accessed | tf_op | source)
XLA Modules:
  0.0 41.7 jit_solution(9792245692587356745)
XLA Ops:
  0.6 0.0 copy-start
  0.6 2.2 %copy-done = f32[128,32,256]{2,1,0:T(8,128)S(1)} copy-done((f32[128,32,256]{2,1,0:T(8,128)S(1)}, f32[128,32,256]{2,1,0:T(8,128)}, u32[]{:S(2)}) %copy-start) | copy-done | bytes 4194328
  2.8 0.0 copy-start.1
  2.8 0.8 %copy-done.1 = f32[64,256]{1,0:T(8,128)S(1)} copy-done((f32[64,256]{1,0:T(8,128)S(1)}, f32[64,256]{1,0:T(8,128)}, u32[]{:S(2)}) %copy-start.1) | copy-done | bytes 65560
  3.7 0.0 copy-start.2
  3.7 0.8 %copy-done.2 = f32[64,128]{1,0:T(8,128)S(1)} copy-done((f32[64,128]{1,0:T(8,128)S(1)}, f32[64,128]{1,0:T(8,128)}, u32[]{:S(2)}) %copy-start.2) | copy-done | bytes 32792
  4.4 0.0 copy-start.3
  4.4 0.7 %copy-done.3 = f32[64,32]{0,1:T(8,128)S(1)} copy-done((f32[64,32]{0,1:T(8,128)S(1)}, f32[64,32]{0,1:T(8,128)}, u32[]{:S(2)}) %copy-start.3) | copy-done | bytes 8216
  5.1 34.7 %shard_map.67 = (f32[64,128]{1,0:T(8,128)S(1)}, f32[32,64]{1,0:T(8,128)S(1)}, f32[64,256]{1,0:T(8,128)S(1)}) custom-call(f32[4096,256]{1,0:T(8,128)S(1)} %bitcast.3, f32[64,128]{1,0:T(8,128)S(1)} %copy-done.2, f32[32,64]{1,0:T(8,128)S(1)} %bitcast.4, f32[64,256]{1,0:T(8,128)S(1)} %copy-done.1), custom_call_target="tpu_custom_call" | custom-call | tf_op jit(solution)/shard_map/pallas_call | solution.py:336
  39.8 0.6 %copy.10 = f32[64,128]{1,0:T(8,128)} copy(f32[64,128]{1,0:T(8,128)S(1)} %get-tuple-element.12) | data formatting | bytes 65536
  40.5 0.6 %copy.11 = f32[64,32]{0,1:T(8,128)} copy(f32[64,32]{0,1:T(8,128)S(1)} %bitcast.5) | data formatting | bytes 16384
  41.1 0.6 %copy.12 = f32[64,256]{1,0:T(8,128)} copy(f32[64,256]{1,0:T(8,128)S(1)} %get-tuple-element.14) | data formatting | bytes 131072
Async XLA Ops:
  0.6 2.2 %copy-start = (f32[128,32,256]{2,1,0:T(8,128)S(1)}, f32[128,32,256]{2,1,0:T(8,128)}, u32[]{:S(2)}) copy-start(f32[128,32,256]{2,1,0:T(8,128)} %param.4) | copy-start | bytes 12582916
  2.8 0.8 %copy-start.1 = (f32[64,256]{1,0:T(8,128)S(1)}, f32[64,256]{1,0:T(8,128)}, u32[]{:S(2)}) copy-start(f32[64,256]{1,0:T(8,128)} %time_hbm.1) | copy-start | bytes 196612
  3.7 0.8 %copy-start.2 = (f32[64,128]{1,0:T(8,128)S(1)}, f32[64,128]{1,0:T(8,128)}, u32[]{:S(2)}) copy-start(f32[64,128]{1,0:T(8,128)} %lon_hbm.1) | copy-start | bytes 98308
  4.4 0.7 %copy-start.3 = (f32[64,32]{0,1:T(8,128)S(1)}, f32[64,32]{0,1:T(8,128)}, u32[]{:S(2)}) copy-start(f32[64,32]{0,1:T(8,128)} %param.6) | copy-start | bytes 24580

commit v3 on v2

--- a/solution.py
+++ b/solution.py
@@ -95,13 +95,6 @@
         return lax.rem(self.me() + (self.count - offset), self.count)
 
 
-def when(condition, action):
-    if condition is True:
-        action()
-    else:
-        pl.when(condition)(action)
-
-
 class Share:
     def __init__(self, group, slots, send, recv):
         self.group, self.slots = group, slots
@@ -128,74 +121,69 @@
 
 
 class Reduce:
-    def __init__(self, group, part, slots, final, send1, recv1, send2, recv2):
-        self.group, self.part, self.slots, self.final = group, part, slots, final
-        pieces = part.shape[0]
-        self.owners = min(group.count, pieces)
-        self.per = pieces // self.owners
-        self.all_own = self.owners == group.count
-        me = group.me()
-        self.scatter, self.gather = [], []
-        for o in range(1, group.count):
-            to = group.peer(o)
-            device = group.device(to)
+    def __init__(self, near, far, part, slots, across, final, *sems):
+        self.near, self.far = near, far
+        self.part, self.slots, self.across, self.final = part, slots, across, final
+        self.per = part.shape[0] // near.count
+        me, here = near.me(), far.me()
+        self.scatter, self.spread, self.gather = [], [], []
+        for o in range(1, near.count):
+            to = near.peer(o)
+            device = near.device(to)
             self.scatter.append(pltpu.make_async_remote_copy(
                 src_ref=part.at[self.tiles(to)], dst_ref=slots.at[o - 1],
-                send_sem=send1.at[o - 1], recv_sem=recv1.at[o - 1],
+                send_sem=sems[0].at[o - 1], recv_sem=sems[1].at[o - 1],
                 device_id=device, device_id_type=MESH))
             self.gather.append(pltpu.make_async_remote_copy(
                 src_ref=final.at[self.tiles(me)], dst_ref=final.at[self.tiles(me)],
-                send_sem=send2.at[o - 1], recv_sem=recv2.at[o - 1],
+                send_sem=sems[4].at[o - 1], recv_sem=sems[5].at[o - 1],
                 device_id=device, device_id_type=MESH))
-
-    def owns(self, index):
-        return True if self.all_own else index < self.owners
+        for o in range(1, far.count):
+            self.spread.append(pltpu.make_async_remote_copy(
+                src_ref=across.at[here], dst_ref=across.at[here],
+                send_sem=sems[2].at[o - 1], recv_sem=sems[3].at[o - 1],
+                device_id=far.device(far.peer(o)), device_id_type=MESH))
 
     def tiles(self, index):
-        if not self.all_own:
-            index = jnp.minimum(index, self.owners - 1)
         return pl.ds(index * self.per, self.per)
 
     def start(self, value):
         for i in range(value.shape[1] // LANE):
             rows = value.shape[0] // SUB
             self.part[i * rows:(i + 1) * rows] = value[:, i * LANE:(i + 1) * LANE].reshape(rows, SUB, LANE)
-        for o, copy in enumerate(self.scatter, 1):
-            when(self.owns(self.group.peer(o)), copy.start)
+        for copy in self.scatter:
+            copy.start()
 
     def middle(self):
-        me = self.group.me()
-
-        def add():
-            for copy in self.scatter:
-                copy.wait_recv()
-            total = self.part[self.tiles(me)]
-            for o in range(1, self.group.count):
-                total = total + self.slots[o - 1]
-            self.final[self.tiles(me)] = total
-            for copy in self.gather:
-                copy.start()
-
-        when(self.owns(me), add)
+        me = self.near.me()
+        for copy in self.scatter:
+            copy.wait_recv()
+        total = self.part[self.tiles(me)]
+        for o in range(1, self.near.count):
+            total = total + self.slots[o - 1]
+        self.across[self.far.me()] = total
+        for copy in self.spread:
+            copy.start()
+        for copy in self.spread:
+            copy.wait_recv()
+        total = self.across[0]
+        for i in range(1, self.far.count):
+            total = total + self.across[i]
+        self.final[self.tiles(me)] = total
+        for copy in self.gather:
+            copy.start()
 
     def finish(self, rank):
-        me = self.group.me()
-        for o, copy in enumerate(self.gather, 1):
-            when(self.owns(self.group.source(o)), copy.wait_recv)
+        for copy in self.gather:
+            copy.wait_recv()
         rows = rank // SUB
         pieces = self.part.shape[0]
         tiles = [self.final[i:i + rows].reshape(rank, LANE) for i in range(0, pieces, rows)]
         return tiles[0] if len(tiles) == 1 else jnp.concatenate(tiles, axis=1)
 
     def drain(self):
-        for o, copy in enumerate(self.scatter, 1):
-            when(self.owns(self.group.peer(o)), copy.wait_send)
-
-        def sent():
-            for copy in self.gather:
-                copy.wait_send()
-
-        when(self.owns(self.group.me()), sent)
+        for copy in self.scatter + self.spread + self.gather:
+            copy.wait_send()
 
 
 def kernel(sizes, shape, x_hbm, lon_hbm, lat_hbm, time_hbm, lon_out, lat_out, time_out,
@@ -216,11 +204,11 @@
     for c in range(n_lon // step):
         piece(c).start()
     lon_axis, lat_axis, tm_axis = (Group(sizes, (a,)) for a in ("lon", "lat", "tm"))
-    lat_tm, lon_tm, lon_lat = Group(sizes, ("lat", "tm")), Group(sizes, ("lon", "tm")), Group(sizes, ("lon", "lat"))
+    lon_tm = Group(sizes, ("lon", "tm"))
 
     barrier = pltpu.get_barrier_semaphore()
     signals = 0
-    for group in (lat_tm, lon_tm, lon_lat):
+    for group in (lon_tm, lat_axis):
         for o in range(1, group.count):
             pl.semaphore_signal(barrier, inc=1, device_id=group.device(group.peer(o)), device_id_type=MESH)
             signals += 1
@@ -232,9 +220,9 @@
     time_gram = Share(tm_axis, *comm[3:6])
     lon_gram = Share(lon_axis, *comm[6:9])
     lat_gram_new = Share(lat_axis, *comm[9:12])
-    lon_sum = Reduce(lat_tm, *comm[12:19])
-    lat_sum = Share(lon_tm, *comm[19:22])
-    time_sum = Reduce(lon_lat, *comm[22:29])
+    lon_sum = Reduce(tm_axis, lat_axis, *comm[12:22])
+    lat_sum = Share(lon_tm, *comm[22:25])
+    time_sum = Reduce(lon_axis, lat_axis, *comm[25:35])
 
     weights = jnp.concatenate(halves(time_ref[...]), axis=0)
     lat_t = lat_ref[...]
@@ -257,7 +245,7 @@
             value.reshape(step, n_lat, rank) * lat_t[None], axis=1)
         return 0
 
-    lax.fori_loop(0, n_lon // step, first, 0)
+    lax.fori_loop(0, n_lon // step, first, 0, unroll=2)
     lon_part = turn(lon_t[...])
     if signals:
         pl.semaphore_wait(barrier, signals)
@@ -278,7 +266,7 @@
         scale = lon_t[pl.ds(pl.multiple_of(c * step, step), step), :]
         return total + jnp.sum(inner[rows, :].reshape(step, n_lat, rank) * scale[:, None, :], axis=0)
 
-    lat_part = lax.fori_loop(0, n_lon // step, second, jnp.zeros((n_lat, rank), jnp.float32))
+    lat_part = lax.fori_loop(0, n_lon // step, second, jnp.zeros((n_lat, rank), jnp.float32), unroll=2)
     lat_sum.start(turn(lat_part))
     lon_g = lon_gram.finish(rank)
     gram = lon_g * time_g
@@ -298,7 +286,7 @@
         total = total + jnp.dot(both, xh[rows, :], preferred_element_type=jnp.float32)
         return total + jnp.dot(both, xl[rows, :], preferred_element_type=jnp.float32)
 
-    both = lax.fori_loop(0, n_lon // step, third, jnp.zeros((2 * rank, n_hr), jnp.float32))
+    both = lax.fori_loop(0, n_lon // step, third, jnp.zeros((2 * rank, n_hr), jnp.float32), unroll=2)
     time_sum.start(both[:rank] + both[rank:])
     time_sum.middle()
     gram = lon_g * lat_gram_new.finish(rank)
@@ -320,18 +308,19 @@
         blocks = max(LANE // columns, 1)
         return [pltpu.VMEM((count, rank // blocks, blocks * columns), jnp.float32)] + sems(count)
 
-    def reduce(count, columns):
+    def reduce(near, far, columns):
         pieces = rank // SUB * -(-columns // LANE)
-        per = pieces // min(count, pieces)
+        per = pieces // near
         return [
             pltpu.VMEM((pieces, SUB, LANE), jnp.float32),
-            pltpu.VMEM((max(count - 1, 1), per, SUB, LANE), jnp.float32),
+            pltpu.VMEM((max(near - 1, 1), per, SUB, LANE), jnp.float32),
+            pltpu.VMEM((far, per, SUB, LANE), jnp.float32),
             pltpu.VMEM((pieces, SUB, LANE), jnp.float32),
-        ] + sems(count) + sems(count)
+        ] + sems(near) + sems(far) + sems(near)
 
     lon, lat, tm = sizes["lon"], sizes["lat"], sizes["tm"]
     comm = share(lat) + share(tm) + share(lon) + share(lat)
-    comm += reduce(lat * tm, n_lon) + share(lon * tm, n_lat) + reduce(lon * lat, n_hr)
+    comm += reduce(tm, lat, n_lon) + share(lon * tm, n_lat) + reduce(lon, lat, n_hr)
     lat_turned = lat_factor.T
     lon_new, lat_new, time_new = pl.pallas_call(
         functools.partial(kernel, sizes, (n_lon, n_lat, n_hr)),
@@ -352,7 +341,7 @@
             pltpu.VMEM(lat_factor.shape, jnp.float32),
         ] + comm,
         compiler_params=pltpu.CompilerParams(
-            collective_id=0, has_side_effects=True, vmem_limit_bytes=40 * 1024 * 1024),
+            collective_id=0, has_side_effects=True, vmem_limit_bytes=63 * 1024 * 1024),
     )(flat, lon_factor, lat_turned, time_factor)
     return lon_new, lat_new.T, time_new
 

time: 42 us -> 42.7 us (1.017)
  Pallas kernels: 34.7 us -> 37.6 us
  local copies, waits for them, and re-layouts: 6.35 us -> 4.17 us
    pallas_call x1, Pallas kernels: 34.7 us -> 37.6 us  [shards(): pl.pallas_call(functools.partial(kernel, sizes, (n_lon, n_lat, n_hr)), ou...]
    unnamed x11 -> x3, local copies, waits for them, and re-layouts: 6.35 us -> 4.17 us
where the time goes in v3:
time: 42.7 us; the launch traced here: 42.4 us
  Pallas kernels  37.6 us (88%)
  local copies, waits for them, and re-layouts  4.17 us (10%)
  between operations  0.64 us (1%)
    pallas_call x1, Pallas kernels, shards(): pl.pallas_call(functools.partial(kernel, sizes, (n_lon, n_lat, n_hr)), ou...  37.6 us
    unnamed x3, local copies, waits for them, and re-layouts  4.17 us

profile of v3, /device:TPU:0, one launch (start us, length us, event | category | flops | bytes accessed | tf_op | source)
XLA Modules:
  0.0 42.4 jit_solution(606882089933958890)
XLA Ops:
  0.6 37.6 %shard_map.67 = (f32[64,128]{1,0:T(8,128)}, f32[32,64]{1,0:T(8,128)}, f32[64,256]{1,0:T(8,128)}) custom-call(f32[4096,256]{1,0:T(8,128)} %bitcast.3, f32[64,128]{1,0:T(8,128)} %lon_hbm.1, f32[32,64]{1,0:T(8,128)} %bitcast.4, f32[64,256]{1,0:T(8,128)} %time_hbm.1), custom_call_target="tpu_custom_call" | custom-call | tf_op jit(solution)/shard_map/pallas_call | solution.py:325
  38.3 1.4 %copy.10 = f32[64,128]{1,0:T(8,128)} copy(f32[64,128]{1,0:T(8,128)} %get-tuple-element.12) | data formatting | bytes 65536
  39.6 1.3 %copy.11 = f32[64,32]{0,1:T(8,128)} copy(f32[64,32]{0,1:T(8,128)} %bitcast.5) | data formatting | bytes 16384
  41.0 1.5 %copy.12 = f32[64,256]{1,0:T(8,128)} copy(f32[64,256]{1,0:T(8,128)} %get-tuple-element.14) | data formatting | bytes 131072

commit v4 on v3

--- a/solution.py
+++ b/solution.py
@@ -187,9 +187,11 @@
 
 
 def kernel(sizes, shape, x_hbm, lon_hbm, lat_hbm, time_hbm, lon_out, lat_out, time_out,
-           x_ref, lon_ref, lat_ref, time_ref, load, x_load, xh, xl, inner, lon_t, lat_new_ref, *comm):
+           lon_ref, lat_ref, time_ref, load, x_load, across, inner, lon_t, lat_new_ref, *rest):
     n_lon, n_lat, n_hr = shape
     rank = lon_ref.shape[0]
+    lanes = n_hr // LANE
+    x_tiles, comm = rest[:lanes], rest[lanes:]
     step = 16
     chunk = step * n_lat
     small = [pltpu.make_async_copy(src, dst, load.at[i]) for i, (src, dst) in enumerate(
@@ -197,12 +199,14 @@
 
     def piece(c):
         rows = pl.ds(pl.multiple_of(c * chunk, chunk), chunk)
-        return pltpu.make_async_copy(x_hbm.at[rows], x_ref.at[rows], x_load.at[c])
+        return [pltpu.make_async_copy(x_hbm.at[rows, pl.ds(t * LANE, LANE)], tile.at[rows], x_load.at[t, c])
+                for t, tile in enumerate(x_tiles)]
 
     for copy in small:
         copy.start()
     for c in range(n_lon // step):
-        piece(c).start()
+        for copy in piece(c):
+            copy.start()
     lon_axis, lat_axis, tm_axis = (Group(sizes, (a,)) for a in ("lon", "lat", "tm"))
     lon_tm = Group(sizes, ("lon", "tm"))
 
@@ -232,10 +236,9 @@
 
     def first(c, _):
         rows = pl.ds(pl.multiple_of(c * chunk, chunk), chunk)
-        piece(c).wait()
-        high, low = halves(x_ref[rows, :])
-        xh[rows, :] = high
-        xl[rows, :] = low
+        for copy in piece(c):
+            copy.wait()
+        high, low = halves(jnp.concatenate([tile[rows, :] for tile in x_tiles], axis=1))
         nt = (((1,), (1,)), ((), ()))
         both = lax.dot_general(high, weights, nt, preferred_element_type=jnp.float32)
         both = both + lax.dot_general(low, weights, nt, preferred_element_type=jnp.float32)
@@ -268,28 +271,33 @@
 
     lat_part = lax.fori_loop(0, n_lon // step, second, jnp.zeros((n_lat, rank), jnp.float32), unroll=2)
     lat_sum.start(turn(lat_part))
+
+    lon_halves = jnp.concatenate(halves(lon_new), axis=0)
+
+    def third(j, _):
+        plane = jnp.concatenate(
+            [tile[pl.ds(j, n_lon, stride=n_lat), :] for tile in x_tiles], axis=1)
+        high, low = halves(plane)
+        both = jnp.dot(lon_halves, high, preferred_element_type=jnp.float32)
+        both = both + jnp.dot(lon_halves, low, preferred_element_type=jnp.float32)
+        across[j] = both[:rank] + both[rank:]
+        return 0
+
+    lax.fori_loop(0, n_lat, third, 0, unroll=2)
     lon_g = lon_gram.finish(rank)
     gram = lon_g * time_g
     hals(lat_new_ref, lat_old, lat_sum.finish(n_lat), gram)
 
     lat_new = lat_new_ref[...]
     lat_gram_new.start(gram_of(lat_new))
-    lat_t = turn(lat_new)
-    lat_out[...] = lat_t
-
-    def third(c, total):
-        rows = pl.ds(pl.multiple_of(c * chunk, chunk), chunk)
-        scale = lon_t[pl.ds(pl.multiple_of(c * step, step), step), :]
-        pairs = (scale[:, None, :] * lat_t[None]).reshape(chunk, rank)
-        high = pairs.astype(jnp.bfloat16).astype(jnp.float32)
-        both = jnp.concatenate([high, pairs - high], axis=1).T.astype(jnp.bfloat16)
-        total = total + jnp.dot(both, xh[rows, :], preferred_element_type=jnp.float32)
-        return total + jnp.dot(both, xl[rows, :], preferred_element_type=jnp.float32)
-
-    both = lax.fori_loop(0, n_lon // step, third, jnp.zeros((2 * rank, n_hr), jnp.float32), unroll=2)
-    time_sum.start(both[:rank] + both[rank:])
+
+    time_part = across[0] * lat_new[:, 0:1]
+    for j in range(1, n_lat):
+        time_part = time_part + across[j] * lat_new[:, j:j + 1]
+    time_sum.start(time_part)
     time_sum.middle()
     gram = lon_g * lat_gram_new.finish(rank)
+    lat_out[...] = turn(lat_new)
     hals(time_out, time_ref[...], time_sum.finish(rank), gram)
     for part in (lon_sum, time_sum):
         part.drain()
@@ -328,20 +336,18 @@
         in_specs=[pl.BlockSpec(memory_space=pltpu.HBM)] * 4,
         out_specs=[pl.BlockSpec(memory_space=pltpu.VMEM)] * 3,
         scratch_shapes=[
-            pltpu.VMEM(flat.shape, jnp.float32),
             pltpu.VMEM(lon_factor.shape, jnp.float32),
             pltpu.VMEM(lat_turned.shape, jnp.float32),
             pltpu.VMEM(time_factor.shape, jnp.float32),
             pltpu.SemaphoreType.DMA((3,)),
-            pltpu.SemaphoreType.DMA((n_lon // 16,)),
-            pltpu.VMEM((cells, n_hr), jnp.bfloat16),
-            pltpu.VMEM((cells, n_hr), jnp.bfloat16),
+            pltpu.SemaphoreType.DMA((n_hr // LANE, n_lon // 16)),
+            pltpu.VMEM((n_lat, rank, n_hr), jnp.float32),
             pltpu.VMEM((cells, rank), jnp.float32),
             pltpu.VMEM((n_lon, rank), jnp.float32),
             pltpu.VMEM(lat_factor.shape, jnp.float32),
-        ] + comm,
+        ] + [pltpu.VMEM((cells, LANE), jnp.float32)] * (n_hr // LANE) + comm,
         compiler_params=pltpu.CompilerParams(
-            collective_id=0, has_side_effects=True, vmem_limit_bytes=63 * 1024 * 1024),
+            collective_id=0, has_side_effects=True, vmem_limit_bytes=61 * 1024 * 1024),
     )(flat, lon_factor, lat_turned, time_factor)
     return lon_new, lat_new.T, time_new
 

time: 42.7 us -> 42.4 us (level)
  no operation moved by 1% of the time
where the time goes in v4:
time: 42.4 us; the launch traced here: 42.1 us
  Pallas kernels  37.3 us (88%)
  local copies, waits for them, and re-layouts  4.17 us (10%)
  between operations  0.64 us (2%)
    pallas_call x1, Pallas kernels, shards(): pl.pallas_call(functools.partial(kernel, sizes, (n_lon, n_lat, n_hr)), ou...  37.3 us
    unnamed x3, local copies, waits for them, and re-layouts  4.17 us

profile of v4, /device:TPU:0, one launch (start us, length us, event | category | flops | bytes accessed | tf_op | source)
XLA Modules:
  0.0 42.1 jit_solution(4876545949617684712)
XLA Ops:
  0.6 37.3 %shard_map.67 = (f32[64,128]{1,0:T(8,128)}, f32[32,64]{1,0:T(8,128)}, f32[64,256]{1,0:T(8,128)}) custom-call(f32[4096,256]{1,0:T(8,128)} %bitcast.3, f32[64,128]{1,0:T(8,128)} %lon_hbm.1, f32[32,64]{1,0:T(8,128)} %bitcast.4, f32[64,256]{1,0:T(8,128)} %time_hbm.1), custom_call_target="tpu_custom_call" | custom-call | tf_op jit(solution)/shard_map/pallas_call | solution.py:333
  38.0 1.4 %copy.10 = f32[64,128]{1,0:T(8,128)} copy(f32[64,128]{1,0:T(8,128)} %get-tuple-element.12) | data formatting | bytes 65536
  39.3 1.3 %copy.11 = f32[64,32]{0,1:T(8,128)} copy(f32[64,32]{0,1:T(8,128)} %bitcast.5) | data formatting | bytes 16384
  40.7 1.5 %copy.12 = f32[64,256]{1,0:T(8,128)} copy(f32[64,256]{1,0:T(8,128)} %get-tuple-element.14) | data formatting | bytes 131072

commit v5 on v4

--- a/solution.py
+++ b/solution.py
@@ -347,7 +347,7 @@
             pltpu.VMEM(lat_factor.shape, jnp.float32),
         ] + [pltpu.VMEM((cells, LANE), jnp.float32)] * (n_hr // LANE) + comm,
         compiler_params=pltpu.CompilerParams(
-            collective_id=0, has_side_effects=True, vmem_limit_bytes=61 * 1024 * 1024),
+            collective_id=0, has_side_effects=True, vmem_limit_bytes=52 * 1024 * 1024),
     )(flat, lon_factor, lat_turned, time_factor)
     return lon_new, lat_new.T, time_new
 

time: 42.4 us -> 40.6 us (0.958)
  Pallas kernels: 37.3 us -> 35.5 us
    pallas_call x1, Pallas kernels: 37.3 us -> 35.5 us  [shards(): pl.pallas_call(functools.partial(kernel, sizes, (n_lon, n_lat, n_hr)), ou...]
    unnamed x3 -> x9, local copies, waits for them, and re-layouts: 4.17 us -> 4.16 us
where the time goes in v5:
time: 40.6 us; the launch traced here: 40.3 us
  Pallas kernels  35.5 us (87%)
  local copies, waits for them, and re-layouts  4.16 us (10%)
  between operations  0.65 us (2%)
    pallas_call x1, Pallas kernels, shards(): pl.pallas_call(functools.partial(kernel, sizes, (n_lon, n_lat, n_hr)), ou...  35.5 us
    unnamed x9, local copies, waits for them, and re-layouts  4.16 us

profile of v5, /device:TPU:0, one launch (start us, length us, event | category | flops | bytes accessed | tf_op | source)
XLA Modules:
  0.0 40.3 jit_solution(3001831027692515492)
XLA Ops:
  0.6 0.0 copy-start
  0.6 0.8 %copy-done = f32[64,256]{1,0:T(8,128)S(1)} copy-done((f32[64,256]{1,0:T(8,128)S(1)}, f32[64,256]{1,0:T(8,128)}, u32[]{:S(2)}) %copy-start) | copy-done | bytes 65560
  1.5 0.0 copy-start.1
  1.5 0.8 %copy-done.1 = f32[64,128]{1,0:T(8,128)S(1)} copy-done((f32[64,128]{1,0:T(8,128)S(1)}, f32[64,128]{1,0:T(8,128)}, u32[]{:S(2)}) %copy-start.1) | copy-done | bytes 32792
  2.2 0.0 copy-start.2
  2.2 0.7 %copy-done.2 = f32[64,32]{0,1:T(8,128)S(1)} copy-done((f32[64,32]{0,1:T(8,128)S(1)}, f32[64,32]{0,1:T(8,128)}, u32[]{:S(2)}) %copy-start.2) | copy-done | bytes 8216
  2.9 35.5 %shard_map.67 = (f32[64,128]{1,0:T(8,128)S(1)}, f32[32,64]{1,0:T(8,128)S(1)}, f32[64,256]{1,0:T(8,128)S(1)}) custom-call(f32[4096,256]{1,0:T(8,128)} %bitcast.5, f32[64,128]{1,0:T(8,128)S(1)} %copy-done.1, f32[32,64]{1,0:T(8,128)S(1)} %bitcast.3, f32[64,256]{1,0:T(8,128)S(1)} %copy-done), custom_call_target="tpu_custom_call" | custom-call | tf_op jit(solution)/shard_map/pallas_call | solution.py:333
  38.5 0.6 %copy.10 = f32[64,128]{1,0:T(8,128)} copy(f32[64,128]{1,0:T(8,128)S(1)} %get-tuple-element.12) | data formatting | bytes 65536
  39.1 0.6 %copy.11 = f32[64,32]{0,1:T(8,128)} copy(f32[64,32]{0,1:T(8,128)S(1)} %bitcast.4) | data formatting | bytes 16384
  39.7 0.6 %copy.12 = f32[64,256]{1,0:T(8,128)} copy(f32[64,256]{1,0:T(8,128)S(1)} %get-tuple-element.14) | data formatting | bytes 131072
Async XLA Ops:
  0.6 0.8 %copy-start = (f32[64,256]{1,0:T(8,128)S(1)}, f32[64,256]{1,0:T(8,128)}, u32[]{:S(2)}) copy-start(f32[64,256]{1,0:T(8,128)} %time_hbm.1) | copy-start | bytes 196612
  1.5 0.8 %copy-start.1 = (f32[64,128]{1,0:T(8,128)S(1)}, f32[64,128]{1,0:T(8,128)}, u32[]{:S(2)}) copy-start(f32[64,128]{1,0:T(8,128)} %lon_hbm.1) | copy-start | bytes 98308
  2.2 0.7 %copy-start.2 = (f32[64,32]{0,1:T(8,128)S(1)}, f32[64,32]{0,1:T(8,128)}, u32[]{:S(2)}) copy-start(f32[64,32]{0,1:T(8,128)} %param.6) | copy-start | bytes 24580

commit v6 on v5

--- a/solution.py
+++ b/solution.py
@@ -186,7 +186,7 @@
             copy.wait_send()
 
 
-def kernel(sizes, shape, x_hbm, lon_hbm, lat_hbm, time_hbm, lon_out, lat_out, time_out,
+def kernel(sizes, shape, x_hbm, both_hbm, lat_hbm, lon_out, lat_out, time_out,
            lon_ref, lat_ref, time_ref, load, x_load, across, inner, lon_t, lat_new_ref, *rest):
     n_lon, n_lat, n_hr = shape
     rank = lon_ref.shape[0]
@@ -195,7 +195,7 @@
     step = 16
     chunk = step * n_lat
     small = [pltpu.make_async_copy(src, dst, load.at[i]) for i, (src, dst) in enumerate(
-        ((time_hbm, time_ref), (lat_hbm, lat_ref), (lon_hbm, lon_ref)))]
+        ((both_hbm.at[:, pl.ds(n_lon, n_hr)], time_ref), (lat_hbm, lat_ref), (both_hbm.at[:, pl.ds(0, n_lon)], lon_ref)))]
 
     def piece(c):
         rows = pl.ds(pl.multiple_of(c * chunk, chunk), chunk)
@@ -333,7 +333,7 @@
     lon_new, lat_new, time_new = pl.pallas_call(
         functools.partial(kernel, sizes, (n_lon, n_lat, n_hr)),
         out_shape=[jax.ShapeDtypeStruct(f.shape, jnp.float32) for f in (lon_factor, lat_turned, time_factor)],
-        in_specs=[pl.BlockSpec(memory_space=pltpu.HBM)] * 4,
+        in_specs=[pl.BlockSpec(memory_space=pltpu.HBM)] * 3,
         out_specs=[pl.BlockSpec(memory_space=pltpu.VMEM)] * 3,
         scratch_shapes=[
             pltpu.VMEM(lon_factor.shape, jnp.float32),
@@ -348,7 +348,7 @@
         ] + [pltpu.VMEM((cells, LANE), jnp.float32)] * (n_hr // LANE) + comm,
         compiler_params=pltpu.CompilerParams(
             collective_id=0, has_side_effects=True, vmem_limit_bytes=52 * 1024 * 1024),
-    )(flat, lon_factor, lat_turned, time_factor)
+    )(flat, jnp.concatenate([lon_factor, time_factor], axis=1), lat_turned)
     return lon_new, lat_new.T, time_new
 
 

time: 40.6 us -> 39.8 us (0.980)
  local copies, waits for them, and re-layouts: 4.16 us -> 2.56 us
  other arithmetic: 0 us -> 0.85 us
    unnamed x9 -> x5, local copies, waits for them, and re-layouts: 4.16 us -> 2.56 us
    concatenate x0 -> x1, other arithmetic: none -> 0.85 us  [shards(): jnp.concatenate([lon_factor, time_factor], axis=1)]
where the time goes in v6:
time: 39.8 us; the launch traced here: 39.5 us
  Pallas kernels  35.4 us (89%)
  local copies, waits for them, and re-layouts  2.56 us (6%)
  other arithmetic  0.85 us (2%)
  between operations  0.65 us (2%)
    pallas_call x1, Pallas kernels, shards(): pl.pallas_call(functools.partial(kernel, sizes, (n_lon, n_lat, n_hr)), ou...  35.4 us
    unnamed x5, local copies, waits for them, and re-layouts  2.56 us
    concatenate x1, other arithmetic, shards(): jnp.concatenate([lon_factor, time_factor], axis=1)  0.85 us

profile of v6, /device:TPU:0, one launch (start us, length us, event | category | flops | bytes accessed | tf_op | source)
XLA Modules:
  0.0 39.5 jit_solution(4094210516646869101)
XLA Ops:
  0.6 0.9 %pad_maximum_fusion.both_hbm = f32[64,384]{1,0:T(8,128)S(1)} fusion(f32[64,256]{1,0:T(8,128)} %param.7, f32[64,128]{1,0:T(8,128)} %param.5), kind=kLoop, calls=%fused_computation | loop fusion | flops 24576 | bytes 196608 | tf_op jit(solution)/shard_map/concatenate | solution.py:351
  1.5 0.0 copy-start
  1.5 0.7 %copy-done = f32[64,32]{0,1:T(8,128)S(1)} copy-done((f32[64,32]{0,1:T(8,128)S(1)}, f32[64,32]{0,1:T(8,128)}, u32[]{:S(2)}) %copy-start) | copy-done | bytes 8216
  2.2 35.4 %shard_map.67 = (f32[64,128]{1,0:T(8,128)S(1)}, f32[32,64]{1,0:T(8,128)S(1)}, f32[64,256]{1,0:T(8,128)S(1)}) custom-call(f32[4096,256]{1,0:T(8,128)} %bitcast.5, f32[64,384]{1,0:T(8,128)S(1)} %pad_maximum_fusion.both_hbm, f32[32,64]{1,0:T(8,128)S(1)} %bitcast.3), custom_call_target="tpu_custom_call" | custom-call | tf_op jit(solution)/shard_map/pallas_call | solution.py:333
  37.7 0.6 %copy.10 = f32[64,128]{1,0:T(8,128)} copy(f32[64,128]{1,0:T(8,128)S(1)} %get-tuple-element.12) | data formatting | bytes 65536
  38.3 0.6 %copy.11 = f32[64,32]{0,1:T(8,128)} copy(f32[64,32]{0,1:T(8,128)S(1)} %bitcast.4) | data formatting | bytes 16384
  38.9 0.6 %copy.12 = f32[64,256]{1,0:T(8,128)} copy(f32[64,256]{1,0:T(8,128)S(1)} %get-tuple-element.14) | data formatting | bytes 131072
Async XLA Ops:
  1.5 0.7 %copy-start = (f32[64,32]{0,1:T(8,128)S(1)}, f32[64,32]{0,1:T(8,128)}, u32[]{:S(2)}) copy-start(f32[64,32]{0,1:T(8,128)} %param.6) | copy-start | bytes 24580

commit v7 on v6

--- a/solution.py
+++ b/solution.py
@@ -248,7 +248,7 @@
             value.reshape(step, n_lat, rank) * lat_t[None], axis=1)
         return 0
 
-    lax.fori_loop(0, n_lon // step, first, 0, unroll=2)
+    lax.fori_loop(0, n_lon // step, first, 0, unroll=4)
     lon_part = turn(lon_t[...])
     if signals:
         pl.semaphore_wait(barrier, signals)
@@ -269,7 +269,7 @@
         scale = lon_t[pl.ds(pl.multiple_of(c * step, step), step), :]
         return total + jnp.sum(inner[rows, :].reshape(step, n_lat, rank) * scale[:, None, :], axis=0)
 
-    lat_part = lax.fori_loop(0, n_lon // step, second, jnp.zeros((n_lat, rank), jnp.float32), unroll=2)
+    lat_part = lax.fori_loop(0, n_lon // step, second, jnp.zeros((n_lat, rank), jnp.float32), unroll=4)
     lat_sum.start(turn(lat_part))
 
     lon_halves = jnp.concatenate(halves(lon_new), axis=0)
@@ -283,7 +283,7 @@
         across[j] = both[:rank] + both[rank:]
         return 0
 
-    lax.fori_loop(0, n_lat, third, 0, unroll=2)
+    lax.fori_loop(0, n_lat, third, 0, unroll=4)
     lon_g = lon_gram.finish(rank)
     gram = lon_g * time_g
     hals(lat_new_ref, lat_old, lat_sum.finish(n_lat), gram)

time: 39.8 us -> 38.3 us (0.962)
  Pallas kernels: 35.4 us -> 34 us
    pallas_call x1, Pallas kernels: 35.4 us -> 34 us  [shards(): pl.pallas_call(functools.partial(kernel, sizes, (n_lon, n_lat, n_hr)), ou...]
where the time goes in v7:
time: 38.3 us; the launch traced here: 38.1 us
  Pallas kernels  34 us (89%)
  local copies, waits for them, and re-layouts  2.56 us (7%)
  other arithmetic  0.85 us (2%)
  between operations  0.65 us (2%)
    pallas_call x1, Pallas kernels, shards(): pl.pallas_call(functools.partial(kernel, sizes, (n_lon, n_lat, n_hr)), ou...  34 us
    unnamed x5, local copies, waits for them, and re-layouts  2.56 us
    concatenate x1, other arithmetic, shards(): jnp.concatenate([lon_factor, time_factor], axis=1)  0.85 us

profile of v7, /device:TPU:0, one launch (start us, length us, event | category | flops | bytes accessed | tf_op | source)
XLA Modules:
  0.0 38.1 jit_solution(5928093405110354335)
XLA Ops:
  0.6 0.9 %pad_maximum_fusion.both_hbm = f32[64,384]{1,0:T(8,128)S(1)} fusion(f32[64,256]{1,0:T(8,128)} %param.7, f32[64,128]{1,0:T(8,128)} %param.5), kind=kLoop, calls=%fused_computation | loop fusion | flops 24576 | bytes 196608 | tf_op jit(solution)/shard_map/concatenate | solution.py:351
  1.5 0.0 copy-start
  1.5 0.7 %copy-done = f32[64,32]{0,1:T(8,128)S(1)} copy-done((f32[64,32]{0,1:T(8,128)S(1)}, f32[64,32]{0,1:T(8,128)}, u32[]{:S(2)}) %copy-start) | copy-done | bytes 8216
  2.2 34.0 %shard_map.67 = (f32[64,128]{1,0:T(8,128)S(1)}, f32[32,64]{1,0:T(8,128)S(1)}, f32[64,256]{1,0:T(8,128)S(1)}) custom-call(f32[4096,256]{1,0:T(8,128)} %bitcast.5, f32[64,384]{1,0:T(8,128)S(1)} %pad_maximum_fusion.both_hbm, f32[32,64]{1,0:T(8,128)S(1)} %bitcast.3), custom_call_target="tpu_custom_call" | custom-call | tf_op jit(solution)/shard_map/pallas_call | solution.py:333
  36.2 0.6 %copy.10 = f32[64,128]{1,0:T(8,128)} copy(f32[64,128]{1,0:T(8,128)S(1)} %get-tuple-element.12) | data formatting | bytes 65536
  36.8 0.6 %copy.11 = f32[64,32]{0,1:T(8,128)} copy(f32[64,32]{0,1:T(8,128)S(1)} %bitcast.4) | data formatting | bytes 16384
  37.4 0.6 %copy.12 = f32[64,256]{1,0:T(8,128)} copy(f32[64,256]{1,0:T(8,128)S(1)} %get-tuple-element.14) | data formatting | bytes 131072
Async XLA Ops:
  1.5 0.7 %copy-start = (f32[64,32]{0,1:T(8,128)S(1)}, f32[64,32]{0,1:T(8,128)}, u32[]{:S(2)}) copy-start(f32[64,32]{0,1:T(8,128)} %param.6) | copy-start | bytes 24580
